TPU v7x, 256 devices: a whole 4x4x8 slice. The times are simulated.
256 devices in a mesh: dom: 128 (over x, z, y), slab: 2 (over core).
Axes of the slice: x: 4, y: 4, z: 8, core: 2. Of those that a mesh axis runs over, the one named last changes fastest.
Arguments:
- positions: float32 [3, 8388608], P(None, ('dom', 'slab')), may hold values from -6 to 6
- velocities: float32 [3, 8388608], P(None, ('dom', 'slab')), may hold values from -6 to 6
- destination: int32 [8388608], P(('dom', 'slab')), may hold values from 0 to 4, as said below
- live_count: int32 [256], P(('dom', 'slab')), may hold values from 24576 to 32768
- ghost_list: int32 [256, 4, 32], P(('dom', 'slab')), may hold values from 0 to 271
- pair_blocks: int32 [256, 512, 2], P(('dom', 'slab')), may hold values from 0 to 671, as said below
- pair_count: int32 [256], P(('dom', 'slab')), may hold values from 128 to 512, as said below
Outputs:
- new_positions: float32 [3, 8912896], P(None, ('dom', 'slab'))
- new_velocities: float32 [3, 8912896], P(None, ('dom', 'slab'))
Inputs may be any that keep to these rules, and one draw needn't show every extreme that they name: `destination`: among the 32768 slots of one device at most 512 carry the same nonzero code, and exactly 512 carry each nonzero code on some devices. `pair_blocks`: the first entry of a pair is an own block; the second indexes the pool: own blocks, then the slab partner's blocks, then ghost blocks by direction and position. `pair_count`: at most 512, reached on some devices.
All inputs are finite; a program needn't handle non-finite values.
Results may differ from a plain program's by a relative error of at most 0.0003.
Values sent between devices are 32-bit elements; how exact they have to be, the bound alone decides.
A program may use at most 64 MiB of HBM per device.

v0:
```python
import functools
import math

import jax
import jax.numpy as jnp
from jax import lax
from jax.experimental import pallas as pl
from jax.experimental.pallas import tpu as pltpu
from jax.sharding import PartitionSpec as P

BLOCK = 128
MOVE = 512
TAIL = 4 * MOVE // BLOCK
UNROLL = 32
MESH = pl.DeviceIdType.MESH
BF = jnp.bfloat16
F32 = jnp.float32

step_size = 0.25
ALPHA = 0.5 * math.log2(math.e)
ROOT = math.sqrt(ALPHA)
CUT = 9.0 * ALPHA
SOFT = 0.05 * ALPHA
KICK = step_size / math.sqrt(BLOCK)
SCALE = ALPHA**1.5 * 2.0**-CUT / CUT**2 / ROOT * KICK


def split3(value):
    high = value.astype(BF).astype(F32)
    rest = value - high
    middle = rest.astype(BF).astype(F32)
    return high, middle, rest - middle


def neighbour(k):
    n_dom = lax.axis_size("dom")
    offset = (1, n_dom - 1, n_dom // 4, n_dom - n_dom // 4)[k]
    return lax.rem(lax.axis_index("dom") + offset, n_dom)


def greet():
    barrier = pltpu.get_barrier_semaphore()
    pl.semaphore_signal(barrier, inc=1, device_id={"slab": 1 - lax.axis_index("slab")}, device_id_type=MESH)
    for k in range(4):
        pl.semaphore_signal(barrier, inc=1, device_id={"dom": neighbour(k)}, device_id_type=MESH)
    pl.semaphore_wait(barrier, 5)


def exchange_kernel(
    pos_ref, vel_ref, dest_ref, live_ref, ghost_ref,
    own_ref, part_ref, gho_ref, vout_ref,
    rhs, ranks, rows, moved, landed, gbuf, send, recv,
):
    n_groups = dest_ref.shape[0]
    partner = {"slab": 1 - lax.axis_index("slab")}
    live = live_ref[0]

    def codes_of(start, size):
        codes = dest_ref[pl.ds(start, size), :]
        slot = (start + lax.broadcasted_iota(jnp.int32, (size, 128), 0)) * 128
        slot = slot + lax.broadcasted_iota(jnp.int32, (size, 128), 1)
        return jnp.where(slot < live, codes, -1)

    row16 = lax.broadcasted_iota(jnp.int32, (16, 128), 0)

    def drift(i, _):
        base = pl.multiple_of(i * 16, 16)
        stay = jnp.where(codes_of(base, 16) == 0, 1.0, 0.0)
        for u in range(16):
            lanes = pl.ds(pl.multiple_of((base + u) * 128, 128), 128)
            p = pos_ref[:, lanes]
            v = vel_ref[:, lanes]
            here = stay[u : u + 1]
            own_ref[base + u, 0:3, :] = (p + step_size * v) * here
            own_ref[base + u, 3:4, :] = here
            vout_ref[base + u] = v * here
        for c in range(3):
            p = jnp.zeros((16, 128), F32)
            v = jnp.zeros((16, 128), F32)
            for u in range(16):
                lanes = pl.ds(pl.multiple_of((base + u) * 128, 128), 128)
                p = jnp.where(row16 == u, pos_ref[c : c + 1, lanes], p)
                v = jnp.where(row16 == u, vel_ref[c : c + 1, lanes], v)
            for f, value in ((c, p + step_size * v), (c + 3, v)):
                for piece, part in enumerate(split3(value)):
                    at = (f * 3 + piece) * 128
                    rhs[pl.ds(base, 16), at : at + 128] = part.astype(BF)
        return 0

    lax.fori_loop(0, n_groups // 16, drift, 0)
    greet()

    def remote(source, target, slot, device):
        return pltpu.make_async_remote_copy(
            src_ref=source,
            dst_ref=target,
            send_sem=send.at[slot],
            recv_sem=recv.at[slot],
            device_id=device,
            device_id_type=MESH,
        )

    body = remote(own_ref.at[pl.ds(0, n_groups)], part_ref.at[pl.ds(0, n_groups)], 0, partner)
    body.start()

    codes = codes_of(0, n_groups)
    lane_r = lax.broadcasted_iota(jnp.int32, (128, 256), 0)
    lane_c = lax.broadcasted_iota(jnp.int32, (128, 256), 1)
    inside_w = jnp.where(lane_r <= lane_c, 1.0, 0.0).astype(BF)
    group_r = lax.broadcasted_iota(jnp.int32, (n_groups, n_groups), 0)
    group_c = lax.broadcasted_iota(jnp.int32, (n_groups, n_groups), 1)
    before_w = jnp.where(group_c < group_r, 1.0, 0.0).astype(BF)
    for k in range(4):
        moving = codes == k + 1
        counted = jnp.dot(jnp.where(moving, 1.0, 0.0).astype(BF), inside_w, preferred_element_type=F32)
        total = counted[:, 128:]
        before = jnp.dot(before_w, total.astype(BF), preferred_element_type=F32)
        rank = (counted[:, :128] + before).astype(jnp.int32) - 1
        ranks[k] = jnp.where(moving, (rank & 127) + 1, 0).astype(F32).astype(BF)
        first = before.T[0:8]
        rows[k, 0:8, :] = first
        rows[k, 8:16, :] = first + total.T[0:8]

    slot_col = lax.broadcasted_iota(jnp.int32, (256, n_groups), 0).astype(F32)
    wanted = ((lax.broadcasted_iota(jnp.int32, (256, 128), 0) & 127) + 1).astype(F32)
    column = lax.broadcasted_iota(jnp.int32, (128, 128), 1)

    def unit(c):
        return jnp.where(column == c, 1.0, 0.0).astype(BF)

    def gather(i, _):
        k = i // 2
        half = i % 2
        at = slot_col + (half * 256).astype(F32)
        hot = jnp.where((at >= rows[k, 0:1, :]) & (at < rows[k, 8:9, :]), 1.0, 0.0).astype(BF)
        match = jnp.dot(hot, ranks[k], preferred_element_type=F32) == wanted
        total = jnp.dot(jnp.where(match, 1.0, 0.0).astype(BF), unit(3), preferred_element_type=F32)
        for f in range(6):
            target = unit(f if f < 3 else f + 1)
            parts = jnp.dot(hot, rhs[:, f * 384 : f * 384 + 384], preferred_element_type=F32)
            chosen = [jnp.where(match, parts[:, 128 * q : 128 * q + 128], 0.0).astype(BF) for q in range(3)]
            total = total + jnp.dot(
                jnp.concatenate(chosen, axis=1),
                jnp.concatenate([target] * 3, axis=0),
                preferred_element_type=F32,
            )
        turned = total.T
        moved[2 * i] = turned[0:8, 0:128]
        moved[2 * i + 1] = turned[0:8, 128:256]
        return 0

    lax.fori_loop(0, 8, gather, 0)
    per = MOVE // BLOCK
    movers = []
    for k in range(4):
        there = pl.ds(per * k, per)
        movers.append(remote(moved.at[there], landed.at[there], 1 + k, {"dom": neighbour(k)}))
        movers[-1].start()
    for copy in movers:
        copy.wait()
    for j in range(TAIL):
        own_ref[n_groups + j] = landed[j, 0:4, :]
        vout_ref[n_groups + j] = landed[j, 4:7, :]
    tail_at = pl.ds(n_groups, TAIL)
    tail = remote(own_ref.at[tail_at], part_ref.at[tail_at], 5, partner)
    tail.start()

    def pick(i, _):
        for u in range(8):
            gbuf[8 * i + u] = own_ref[ghost_ref[8 * i + u]]
        return 0

    n_ghost = gbuf.shape[0]
    lax.fori_loop(0, n_ghost // 8, pick, 0)
    ghosts = []
    for k in range(4):
        there = pl.ds(n_ghost // 4 * k, n_ghost // 4)
        ghosts.append(remote(gbuf.at[there], gho_ref.at[there], 6 + k, {"dom": neighbour(k)}))
        ghosts[-1].start()
    for copy in ghosts:
        copy.wait()
    body.wait()
    tail.wait()


def features(block, row):
    pos = jnp.where(row < 3, jnp.concatenate([block, jnp.zeros_like(block)], axis=0) * ROOT, 0.0)
    return pos, jnp.sum(pos * pos, axis=0, keepdims=True), block[3:4]


def pair_kernel(pairs_ref, count_ref, own_ref, part_ref, gho_ref, acc_ref, pool, sems):
    n_own = own_ref.shape[0]
    copies = []
    start = 0
    for i, ref in enumerate((own_ref, part_ref, gho_ref)):
        copies.append(pltpu.make_async_copy(ref, pool.at[pl.ds(start, ref.shape[0])], sems.at[i]))
        copies[-1].start()
        start += ref.shape[0]
    acc_ref[...] = jnp.zeros_like(acc_ref)
    for copy in copies:
        copy.wait()
    row = lax.broadcasted_iota(jnp.int32, (8, 128), 0)
    lane = lax.broadcasted_iota(jnp.int32, (128, 128), 1)
    count = count_ref[0]
    npair = pairs_ref.shape[0] // 2
    blank = jnp.zeros((8, 128), F32)

    def group(p0):
        items, fars = [], []
        for u in range(4):
            p = p0 + u
            a = pairs_ref[p]
            b = pairs_ref[npair + p]
            pa, na, wa = features(pool[a], row)
            pb, nb, wb = features(pool[b], row)
            near = jnp.where(row < 3, 2.0 * pa, jnp.where(row == 3, -1.0, jnp.where(row == 4, CUT - na, jnp.where(row == 5, wa, 0.0))))
            far = jnp.where(row < 3, pb, jnp.where(row == 3, nb, jnp.where(row == 4, 1.0, jnp.where(row == 7, wb, 0.0))))
            ah, am, al = split3(near)
            bh, bm, bl = split3(far)
            left = jnp.concatenate([ah, ah, ah, am, am, al], axis=0)
            right = jnp.concatenate([bh, bm, bl, bh, bm, bh], axis=0).astype(BF)
            near_f = jnp.concatenate([ah, am, al, blank], axis=0).astype(BF)
            fars += [bh, bm, bl, blank]
            items.append((p, a, b, pa, wa, pb, wb, left, right, near_f))
        far_t = jnp.concatenate(fars, axis=0).T.astype(BF)
        out, strengths, weights = [], [], []
        for u, (p, a, b, pa, wa, pb, wb, left, right, near_f) in enumerate(items):
            raw = jnp.dot(left.T.astype(BF), right, preferred_element_type=F32)
            taper = jnp.maximum(raw, 0.0)
            inv = lax.rsqrt((CUT + SOFT) - raw)
            ratio = taper * inv
            s = (ratio * ratio) * (inv * jnp.exp2(taper))
            high = s.astype(BF)
            low = (s - high.astype(F32)).astype(BF)
            mine = jnp.where((lane >= 32 * u) & (lane < 32 * u + 32), far_t, jnp.zeros_like(far_t))
            strengths += [high, low]
            weights += [mine, mine]
            g = jnp.dot(
                jnp.concatenate([near_f, near_f], axis=1),
                jnp.concatenate([high, low], axis=0),
                preferred_element_type=F32,
            )
            g = g[0:8] + g[8:16] + g[16:24]
            on = jnp.where(p < count, SCALE, 0.0)
            out.append([a, b, None, ((0.5 * g - pb * g[5:6]) * (wb * on))[:4]])
        g_near = jnp.dot(
            jnp.concatenate(strengths, axis=1),
            jnp.concatenate(weights, axis=0),
            preferred_element_type=F32,
        ).T
        for u, (p, a, b, pa, wa, pb, wb, left, right, near_f) in enumerate(items):
            g = g_near[32 * u : 32 * u + 8] + g_near[32 * u + 8 : 32 * u + 16] + g_near[32 * u + 16 : 32 * u + 24]
            on = jnp.where(p < count, SCALE, 0.0)
            out[u][2] = ((g - pa * g[7:8]) * (wa * on))[:4]
        return out

    def turn(t, _):
        found = []
        for g in range(UNROLL // 4):
            found += group(t * UNROLL + 4 * g)
        for a, b, on_near, on_far in found:
            acc_ref[a] += on_near
            acc_ref[b] += on_far
        return 0

    lax.fori_loop(0, (count + UNROLL - 1) // UNROLL, turn, 0)


def return_kernel(acc_ref, pret_ref, gret_ref, send, recv):
    n_own = pret_ref.shape[0]
    per = gret_ref.shape[0] // 4
    greet()
    copies = [
        pltpu.make_async_remote_copy(
            src_ref=acc_ref.at[pl.ds(n_own, n_own)],
            dst_ref=pret_ref,
            send_sem=send.at[0],
            recv_sem=recv.at[0],
            device_id={"slab": 1 - lax.axis_index("slab")},
            device_id_type=MESH,
        )
    ]
    for k in range(4):
        copies.append(
            pltpu.make_async_remote_copy(
                src_ref=acc_ref.at[pl.ds(2 * n_own + per * k, per)],
                dst_ref=gret_ref.at[pl.ds(per * k, per)],
                send_sem=send.at[1 + k],
                recv_sem=recv.at[1 + k],
                device_id={"dom": neighbour(k ^ 1)},
                device_id_type=MESH,
            )
        )
    for copy in copies:
        copy.start()
    for copy in copies:
        copy.wait()


def finish_kernel(ghost_ref, own_ref, vel_ref, acc_ref, pret_ref, gret_ref, npos_ref, nvel_ref, total):
    n_own = own_ref.shape[0]
    total[...] = acc_ref[...] + pret_ref[...]

    def back(i, _):
        for u in range(8):
            total[ghost_ref[8 * i + u]] += gret_ref[8 * i + u]
        return 0

    lax.fori_loop(0, gret_ref.shape[0] // 8, back, 0)

    def write(i, _):
        for u in range(16):
            b = i * 16 + u
            lanes = pl.ds(pl.multiple_of(b * 128, 128), 128)
            npos_ref[:, lanes] = own_ref[b, 0:3, :]
            nvel_ref[:, lanes] = vel_ref[b] + total[b, 0:3, :]
        return 0

    lax.fori_loop(0, n_own // 16, write, 0)


def shards(positions, velocities, destination, live_count, ghost_list, pair_blocks, pair_count):
    n_rows = positions.shape[1]
    n_groups = n_rows // BLOCK
    n_own = n_groups + TAIL
    n_ghost = 4 * ghost_list.shape[2]
    n_pool = 2 * n_own + n_ghost
    smem = pl.BlockSpec(memory_space=pltpu.SMEM)
    vmem = pl.BlockSpec(memory_space=pltpu.VMEM)
    anywhere = pl.BlockSpec(memory_space=pl.ANY)
    ghost_flat = ghost_list.reshape(n_ghost)
    pairs = pair_blocks[0].T.reshape(2 * pair_blocks.shape[1])

    own, part, gho, vel = pl.pallas_call(
        exchange_kernel,
        out_shape=(
            jax.ShapeDtypeStruct((n_own, 4, BLOCK), F32),
            jax.ShapeDtypeStruct((n_own, 4, BLOCK), F32),
            jax.ShapeDtypeStruct((n_ghost, 4, BLOCK), F32),
            jax.ShapeDtypeStruct((n_own, 3, BLOCK), F32),
        ),
        in_specs=[vmem, vmem, vmem, smem, smem],
        out_specs=(vmem, vmem, vmem, vmem),
        scratch_shapes=[
            pltpu.VMEM((n_groups, 18 * BLOCK), BF),
            pltpu.VMEM((4, n_groups, BLOCK), BF),
            pltpu.VMEM((4, 16, n_groups), F32),
            pltpu.VMEM((TAIL, 8, BLOCK), F32),
            pltpu.VMEM((TAIL, 8, BLOCK), F32),
            pltpu.VMEM((n_ghost, 4, BLOCK), F32),
            pltpu.SemaphoreType.DMA((10,)),
            pltpu.SemaphoreType.DMA((10,)),
        ],
        compiler_params=pltpu.CompilerParams(
            collective_id=0, has_side_effects=True, vmem_limit_bytes=48 << 20
        ),
        name="exchange",
    )(positions, velocities, destination.reshape(n_groups, BLOCK), live_count, ghost_flat)

    acc = pl.pallas_call(
        pair_kernel,
        out_shape=jax.ShapeDtypeStruct((n_pool, 4, BLOCK), F32),
        in_specs=[smem, smem, anywhere, anywhere, anywhere],
        out_specs=vmem,
        scratch_shapes=[
            pltpu.VMEM((n_pool, 4, BLOCK), F32),
            pltpu.SemaphoreType.DMA((3,)),
        ],
        compiler_params=pltpu.CompilerParams(vmem_limit_bytes=48 << 20),
        name="pairs",
    )(pairs, pair_count, own, part, gho)

    pret, gret = pl.pallas_call(
        return_kernel,
        out_shape=(
            jax.ShapeDtypeStruct((n_own, 4, BLOCK), F32),
            jax.ShapeDtypeStruct((n_ghost, 4, BLOCK), F32),
        ),
        in_specs=[anywhere],
        out_specs=(anywhere, anywhere),
        scratch_shapes=[pltpu.SemaphoreType.DMA((5,)), pltpu.SemaphoreType.DMA((5,))],
        compiler_params=pltpu.CompilerParams(collective_id=1, has_side_effects=True),
        name="returns",
    )(acc)

    whole = lambda *shape: pl.BlockSpec(shape, lambda i: (0,) * len(shape))
    return pl.pallas_call(
        finish_kernel,
        grid=(1,),
        out_shape=(
            jax.ShapeDtypeStruct((3, n_own * BLOCK), F32),
            jax.ShapeDtypeStruct((3, n_own * BLOCK), F32),
        ),
        in_specs=[
            smem,
            whole(n_own, 4, BLOCK),
            whole(n_own, 3, BLOCK),
            whole(n_own, 4, BLOCK),
            whole(n_own, 4, BLOCK),
            whole(n_ghost, 4, BLOCK),
        ],
        out_specs=(whole(3, n_own * BLOCK), whole(3, n_own * BLOCK)),
        scratch_shapes=[pltpu.VMEM((n_own, 4, BLOCK), F32)],
        compiler_params=pltpu.CompilerParams(vmem_limit_bytes=48 << 20),
        name="finish",
    )(ghost_flat, own, vel, acc, pret, gret)


def solution(mesh):
    return jax.shard_map(
        shards,
        mesh=mesh,
        in_specs=(
            P(None, ("dom", "slab")),
            P(None, ("dom", "slab")),
            P(("dom", "slab")),
            P(("dom", "slab")),
            P(("dom", "slab"), None, None),
            P(("dom", "slab"), None, None),
            P(("dom", "slab")),
        ),
        out_specs=(P(None, ("dom", "slab")), P(None, ("dom", "slab"))),
        check_vma=False,
    )
```

profile of v0, /device:TPU:1, one launch (start us, length us, event | category | flops | bytes accessed | tf_op | source)
XLA Modules:
  0.0 84.7 jit_solution(11731889269184666548)
XLA Ops:
  1.9 0.8 reshape.13.ghost_ref
  2.7 0.7 copy.9
  3.4 0.0 copy-start.3
  3.4 1.0 %copy-done.3 = f32[3,32768]{1,0:T(4,128)S(1)} copy-done((f32[3,32768]{1,0:T(4,128)S(1)}, f32[3,32768]{1,0:T(4,128)}, u32[]{:S(2)}) %copy-start.3) | copy-done | bytes 393240
  4.4 0.0 copy-start.4
  4.4 1.0 %copy-done.4 = f32[3,32768]{1,0:T(4,128)S(1)} copy-done((f32[3,32768]{1,0:T(4,128)S(1)}, f32[3,32768]{1,0:T(4,128)}, u32[]{:S(2)}) %copy-start.4) | copy-done | bytes 393240
  5.5 0.0 copy-start.6
  5.5 0.9 %copy-done.6 = s32[32768]{0:T(1024)S(1)} copy-done((s32[32768]{0:T(1024)S(1)}, s32[32768]{0:T(1024)}, u32[]{:S(2)}) %copy-start.6) | copy-done | bytes 131096
  6.4 34.4 %exchange.1 = (f32[272,4,128]{2,1,0:T(4,128)S(1)}, f32[272,4,128]{2,1,0:T(4,128)S(1)}, f32[128,4,128]{2,1,0:T(4,128)S(1)}, f32[272,3,128]{2,1,0:T(4,128)S(1)}) custom-call(f32[3,32768]{1,0:T(4,128)S(1)} %copy-done.3, f32[3,32768]{1,0:T(4,128)S(1)} %copy-done.4, s32[256,128]{1,0:T(8,128)S(1)} %bitcast.6, s32[1]{0:T(128)S(6)} %copy.10.live_ref, ...), custom_call_target="tpu_custom_call" | custom-call | tf_op jit(solution)/shard_map/exchange/pallas_call | solution.py:334
  40.8 19.6 %pairs.1.acc_ref = f32[672,4,128]{2,1,0:T(4,128)S(1)} custom-call(s32[1024]{0:T(1024)S(1)} %bitcast.7, s32[1]{0:T(128)S(6)} %copy.11.count_ref, f32[272,4,128]{2,1,0:T(4,128)S(1)} %get-tuple-element.8.own_ref, f32[272,4,128]{2,1,0:T(4,128)S(1)} %get-tuple-element.10.part_ref, f32[128,4,128]{2,1,0:T(4,128)S(1)} %get-tuple-element.11.gho_ref), custom_call_target="tpu_custom_call" | custom-call | tf_op jit(solution)/shard_map/pairs/pallas_call | solution.py:360
  60.4 0.0 copy-start
  60.4 1.1 %copy-done = f32[672,4,128]{2,1,0:T(4,128)} copy-done((f32[672,4,128]{2,1,0:T(4,128)}, f32[672,4,128]{2,1,0:T(4,128)S(1)}, u32[]{:S(2)}) %copy-start) | copy-done | bytes 1376280
  61.5 17.3 %returns.1 = (f32[272,4,128]{2,1,0:T(4,128)}, f32[128,4,128]{2,1,0:T(4,128)}) custom-call(f32[672,4,128]{2,1,0:T(4,128)} %copy-done), custom_call_target="tpu_custom_call" | custom-call | tf_op jit(solution)/shard_map/returns/pallas_call | solution.py:373
  78.8 0.0 copy-start.1
  78.8 1.3 %copy-done.1 = f32[672,4,128]{2,1,0:T(4,128)S(1)} copy-done((f32[672,4,128]{2,1,0:T(4,128)S(1)}, f32[672,4,128]{2,1,0:T(4,128)}, u32[]{:S(2)}) %copy-start.1) | copy-done | bytes 1376280
  80.2 0.0 copy-start.2
  80.2 1.1 %copy-done.2 = f32[272,4,128]{2,1,0:T(4,128)S(1)} copy-done((f32[272,4,128]{2,1,0:T(4,128)S(1)}, f32[272,4,128]{2,1,0:T(4,128)}, u32[]{:S(2)}) %copy-start.2) | copy-done | bytes 557080
  81.2 0.0 copy-start.5
  81.2 0.9 %copy-done.5 = f32[128,4,128]{2,1,0:T(4,128)S(1)} copy-done((f32[128,4,128]{2,1,0:T(4,128)S(1)}, f32[128,4,128]{2,1,0:T(4,128)}, u32[]{:S(2)}) %copy-start.5) | copy-done | bytes 262168
  82.2 2.5 %finish.1 = (f32[3,34816]{1,0:T(4,128)}, f32[3,34816]{1,0:T(4,128)}) custom-call(s32[128]{0:T(128)S(1)} %reshape.13.ghost_ref, f32[272,4,128]{2,1,0:T(4,128)S(1)} %get-tuple-element.8.own_ref, f32[272,3,128]{2,1,0:T(4,128)S(1)} %get-tuple-element.9.vel_ref, f32[672,4,128]{2,1,0:T(4,128)S(1)} %copy-done.1, f32[272,4,128]{2,1,0:T(4,128)S(1)} %copy-done.2, ...), custom_call_target="tpu_custom_call" | custom-call | tf_op jit(solution)/shard_map/finish/pallas_call | solution.py:387
Async XLA Ops:
  3.4 1.0 %copy-start.3 = (f32[3,32768]{1,0:T(4,128)S(1)}, f32[3,32768]{1,0:T(4,128)}, u32[]{:S(2)}) copy-start(f32[3,32768]{1,0:T(4,128)} %pos_ref.1) | copy-start | bytes 1179652
  4.4 1.0 %copy-start.4 = (f32[3,32768]{1,0:T(4,128)S(1)}, f32[3,32768]{1,0:T(4,128)}, u32[]{:S(2)}) copy-start(f32[3,32768]{1,0:T(4,128)} %vel_ref.1) | copy-start | bytes 1179652
  5.5 0.9 %copy-start.6 = (s32[32768]{0:T(1024)S(1)}, s32[32768]{0:T(1024)}, u32[]{:S(2)}) copy-start(s32[32768]{0:T(1024)} %param.9) | copy-start | bytes 393220
  60.4 1.1 %copy-start = (f32[672,4,128]{2,1,0:T(4,128)}, f32[672,4,128]{2,1,0:T(4,128)S(1)}, u32[]{:S(2)}) copy-start(f32[672,4,128]{2,1,0:T(4,128)S(1)} %pairs.1.acc_ref) | copy-start | bytes 4128772
  78.8 1.3 %copy-start.1 = (f32[672,4,128]{2,1,0:T(4,128)S(1)}, f32[672,4,128]{2,1,0:T(4,128)}, u32[]{:S(2)}) copy-start(f32[672,4,128]{2,1,0:T(4,128)} %copy-done) | copy-start | bytes 4128772
  80.2 1.1 %copy-start.2 = (f32[272,4,128]{2,1,0:T(4,128)S(1)}, f32[272,4,128]{2,1,0:T(4,128)}, u32[]{:S(2)}) copy-start(f32[272,4,128]{2,1,0:T(4,128)} %get-tuple-element.12.pret_ref) | copy-start | bytes 1671172
  81.2 0.9 %copy-start.5 = (f32[128,4,128]{2,1,0:T(4,128)S(1)}, f32[128,4,128]{2,1,0:T(4,128)}, u32[]{:S(2)}) copy-start(f32[128,4,128]{2,1,0:T(4,128)} %get-tuple-element.13.gret_ref) | copy-start | bytes 786436
where the time goes:
time: 85 us; the launch traced here: 84.7 us
  Pallas kernels  73.8 us (87%)
  local copies, waits for them, and re-layouts  8.87 us (10%)
  between operations  1.97 us (2%)
    pallas_call x1, Pallas kernels, shards(): pl.pallas_call(exchange_kernel, out_shape=(jax.ShapeDtypeStruct((n_own, 4...  34.4 us
    pallas_call x1, Pallas kernels, shards(): pl.pallas_call(pair_kernel, out_shape=jax.ShapeDtypeStruct((n_pool, 4, BL...  19.6 us
    pallas_call x1, Pallas kernels, shards(): pl.pallas_call(return_kernel, out_shape=(jax.ShapeDtypeStruct((n_own, 4,...  17.3 us
    unnamed x15, local copies, waits for them, and re-layouts  8.11 us
    pallas_call x1, Pallas kernels, shards(): pl.pallas_call(finish_kernel, grid=(1,), out_shape=(jax.ShapeDtypeStruct(...  2.5 us

commit v1 on v0

v1 whole, which is shorter than its diff:
```python
import functools
import math

import jax
import jax.numpy as jnp
from jax import lax
from jax.experimental import pallas as pl
from jax.experimental.pallas import tpu as pltpu
from jax.sharding import PartitionSpec as P

BLOCK = 128
MOVE = 512
TAIL = 4 * MOVE // BLOCK
GROUP = 8
MESH = pl.DeviceIdType.MESH
BF = jnp.bfloat16
F32 = jnp.float32

step_size = 0.25
ALPHA = 0.5 * math.log2(math.e)
ROOT = math.sqrt(ALPHA)
CUT = 9.0 * ALPHA
SOFT = 0.05 * ALPHA
KICK = step_size / math.sqrt(BLOCK)
SCALE = ALPHA**1.5 * 2.0**-CUT / CUT**2 / ROOT * KICK


def split3(value):
    high = value.astype(BF).astype(F32)
    rest = value - high
    middle = rest.astype(BF).astype(F32)
    return high, middle, rest - middle


def neighbour(k):
    n_dom = lax.axis_size("dom")
    offset = (1, n_dom - 1, n_dom // 4, n_dom - n_dom // 4)[k]
    return lax.rem(lax.axis_index("dom") + offset, n_dom)


def greet():
    barrier = pltpu.get_barrier_semaphore()
    pl.semaphore_signal(barrier, inc=1, device_id={"slab": 1 - lax.axis_index("slab")}, device_id_type=MESH)
    for k in range(4):
        pl.semaphore_signal(barrier, inc=1, device_id={"dom": neighbour(k)}, device_id_type=MESH)
    pl.semaphore_wait(barrier, 5)


def exchange_kernel(
    pos_hbm, vel_hbm, dest_hbm, live_ref, ghost_ref,
    pool_ref, vout_ref,
    pos_ref, vel_ref, dest_ref, own, main, extra, ranks, spans, moved, landed, gbuf, local, send, recv,
):
    n_groups = dest_ref.shape[0]
    n_own = own.shape[0]
    n_ghost = gbuf.shape[0]
    partner = {"slab": 1 - lax.axis_index("slab")}
    live = live_ref[0]
    loads = []
    for i, (source, target) in enumerate(((dest_hbm, dest_ref), (pos_hbm, pos_ref), (vel_hbm, vel_ref))):
        loads.append(pltpu.make_async_copy(source, target, local.at[i]))
        loads[-1].start()
    greet()

    def codes_of(start, size):
        codes = dest_ref[pl.ds(start, size), :]
        slot = (start + lax.broadcasted_iota(jnp.int32, (size, 128), 0)) * 128
        slot = slot + lax.broadcasted_iota(jnp.int32, (size, 128), 1)
        return jnp.where(slot < live, codes, -1)

    row16 = lax.broadcasted_iota(jnp.int32, (16, 128), 0)

    def drift(i, _):
        base = pl.multiple_of(i * 16, 16)
        stay = jnp.where(codes_of(base, 16) == 0, 1.0, 0.0)
        for u in range(16):
            lanes = pl.ds(pl.multiple_of((base + u) * 128, 128), 128)
            p = pos_ref[:, lanes]
            v = vel_ref[:, lanes]
            here = stay[u : u + 1]
            kept = (p + step_size * v) * here
            own[base + u, 0:3, :] = kept
            own[base + u, 3:4, :] = here
            pool_ref[base + u, 0:3, :] = kept
            pool_ref[base + u, 3:4, :] = here
            vout_ref[base + u] = v * here
        for c in range(3):
            p = jnp.zeros((16, 128), F32)
            v = jnp.zeros((16, 128), F32)
            for u in range(16):
                lanes = pl.ds(pl.multiple_of((base + u) * 128, 128), 128)
                p = jnp.where(row16 == u, pos_ref[c : c + 1, lanes], p)
                v = jnp.where(row16 == u, vel_ref[c : c + 1, lanes], v)
            high, middle, low = split3(p + step_size * v)
            main[c, pl.ds(base, 16), 0:128] = high.astype(BF)
            main[c, pl.ds(base, 16), 128:256] = middle.astype(BF)
            extra[c, pl.ds(base, 16), :] = low.astype(BF)
            high, middle, _ = split3(v)
            main[3 + c, pl.ds(base, 16), 0:128] = high.astype(BF)
            main[3 + c, pl.ds(base, 16), 128:256] = middle.astype(BF)
        return 0

    for load in loads:
        load.wait()
    lax.fori_loop(0, n_groups // 16, drift, 0)

    def remote(source, target, slot, device):
        return pltpu.make_async_remote_copy(
            src_ref=source,
            dst_ref=target,
            send_sem=send.at[slot],
            recv_sem=recv.at[slot],
            device_id=device,
            device_id_type=MESH,
        )

    body = remote(own.at[pl.ds(0, n_groups)], pool_ref.at[pl.ds(n_own, n_groups)], 0, partner)
    body.start()

    codes = codes_of(0, n_groups)
    lane_r = lax.broadcasted_iota(jnp.int32, (128, 256), 0)
    lane_c = lax.broadcasted_iota(jnp.int32, (128, 256), 1)
    inside_w = jnp.where(lane_r <= lane_c, 1.0, 0.0).astype(BF)
    group_r = lax.broadcasted_iota(jnp.int32, (n_groups, n_groups), 0)
    group_c = lax.broadcasted_iota(jnp.int32, (n_groups, n_groups), 1)
    before_w = jnp.where(group_c < group_r, 1.0, 0.0).astype(BF)
    for k in range(4):
        moving = codes == k + 1
        counted = jnp.dot(jnp.where(moving, 1.0, 0.0).astype(BF), inside_w, preferred_element_type=F32)
        total = counted[:, 128:]
        before = jnp.dot(before_w, total.astype(BF), preferred_element_type=F32)
        rank = (counted[:, :128] + before).astype(jnp.int32) - 1
        ranks[k] = jnp.where(moving, (rank & 127) + 1, 0).astype(F32).astype(BF).T
        spans[k, 0] = before
        spans[k, 1] = before + total

    slot = lax.broadcasted_iota(jnp.int32, (n_groups, 256), 1).astype(F32)
    wanted = ((lax.broadcasted_iota(jnp.int32, (128, 256), 1) & 127) + 1).astype(F32)

    def gather(i, _):
        k = i // 2
        at = slot + ((i % 2) * 256).astype(F32)
        first, last = spans[k, 0], spans[k, 1]
        here = (at >= jnp.concatenate([first, first], axis=1)) & (at < jnp.concatenate([last, last], axis=1))
        hot = jnp.where(here, 1.0, 0.0)
        found = jnp.dot(ranks[k], hot.astype(BF), preferred_element_type=F32)
        lane = jnp.where(found == wanted, 1.0, 0.0).astype(BF)
        twice = jnp.concatenate([lane, lane], axis=0)

        def put(f, value):
            moved[2 * i, f : f + 1, :] = value[:, :128]
            moved[2 * i + 1, f : f + 1, :] = value[:, 128:]

        for f in range(6):
            fields = jnp.dot(main[f], twice, preferred_element_type=F32)
            if f < 3:
                fields = fields + jnp.dot(extra[f], lane, preferred_element_type=F32)
            put(f if f < 3 else f + 1, jnp.sum(jnp.where(here, fields, 0.0), axis=0, keepdims=True))
        put(3, jnp.sum(hot, axis=0, keepdims=True))
        put(7, jnp.zeros((1, 256), F32))
        return 0

    lax.fori_loop(0, 8, gather, 0)
    per = MOVE // BLOCK
    movers = []
    for k in range(4):
        there = pl.ds(per * k, per)
        movers.append(remote(moved.at[there], landed.at[there], 1 + k, {"dom": neighbour(k)}))
        movers[-1].start()
    for copy in movers:
        copy.wait()
    for j in range(TAIL):
        own[n_groups + j] = landed[j, 0:4, :]
        pool_ref[n_groups + j] = landed[j, 0:4, :]
        vout_ref[n_groups + j] = landed[j, 4:7, :]
    tail = remote(own.at[pl.ds(n_groups, TAIL)], pool_ref.at[pl.ds(n_own + n_groups, TAIL)], 5, partner)
    tail.start()
    per = n_ghost // 4
    ghosts = []
    for k in range(4):

        def pick(i, _):
            for u in range(8):
                gbuf[per * k + 8 * i + u] = own[ghost_ref[k, 8 * i + u]]
            return 0

        lax.fori_loop(0, per // 8, pick, 0)
        there = pl.ds(2 * n_own + per * k, per)
        ghosts.append(remote(gbuf.at[pl.ds(per * k, per)], pool_ref.at[there], 6 + k, {"dom": neighbour(k)}))
        ghosts[-1].start()
    for copy in ghosts:
        copy.wait()
    body.wait()
    tail.wait()


def features(block, row):
    pos = jnp.where(row < 3, jnp.concatenate([block, jnp.zeros_like(block)], axis=0) * ROOT, 0.0)
    return pos, jnp.sum(pos * pos, axis=0, keepdims=True), block[3:4]


def pair_kernel(pairs_ref, count_ref, pool, acc_ref, lefts, rights, nears, highs, lows):
    acc_ref[...] = jnp.zeros_like(acc_ref)
    rights[...] = jnp.zeros_like(rights)
    row = lax.broadcasted_iota(jnp.int32, (8, 128), 0)
    count = count_ref[0]
    npair = pairs_ref.shape[1]

    def cat(parts, axis):
        return jnp.concatenate(parts, axis=axis)

    def blocks_of(p):
        p = jnp.clip(p, 0, npair - 1)
        return pairs_ref[0, p], pairs_ref[1, p]

    def prepare(t, slot):
        left = []
        for u in range(GROUP):
            a, b = blocks_of(t * GROUP + u)
            pa, na, wa = features(pool[a], row)
            pb, nb, wb = features(pool[b], row)
            near = jnp.where(row < 3, 2.0 * pa, jnp.where(row == 3, -1.0, jnp.where(row == 4, CUT - na, jnp.where(row == 5, wa, 0.0))))
            far = jnp.where(row < 3, pb, jnp.where(row == 3, nb, jnp.where(row == 4, 1.0, jnp.where(row == 7, wb, 0.0))))
            ah, am, al = split3(near)
            bh, bm, bl = split3(far)
            v = u % 2
            left.append(cat([ah, ah, ah, am, am, al], 0).astype(BF))
            right = cat([bh, bm, bl, bh, bm, bh], 0).astype(BF)
            rights[slot, u // 2, 48 * v : 48 * v + 48, 128 * v : 128 * v + 128] = right
            nears[slot, u] = cat([ah, am, al, bh, bm, bl], 0).astype(BF)
        for c in range(GROUP // 2):
            lefts[slot, c] = cat(left[2 * c : 2 * c + 2], 0).T

    def strengths(slot):
        for c in range(GROUP // 2):
            raw = jnp.dot(lefts[slot, c], rights[slot, c], preferred_element_type=F32)
            inv = lax.rsqrt((CUT + SOFT) - raw)
            ratio = jnp.maximum(raw, 0.0) * inv
            s = (ratio * ratio) * (inv * jnp.exp2(raw))
            high = s.astype(BF)
            highs[slot, :, 256 * c : 256 * c + 256] = high
            lows[slot, :, 256 * c : 256 * c + 256] = (s - high.astype(F32)).astype(BF)

    def sums(t, slot):
        found = []
        for u in range(GROUP):
            p = t * GROUP + u
            a, b = blocks_of(p)
            xa, xb = pool[a], pool[b]
            lanes = slice(128 * u, 128 * u + 128)
            high, low = highs[slot, :, lanes], lows[slot, :, lanes]
            f = nears[slot, u]
            both = jnp.dot(
                cat([f, f], 1),
                cat([cat([high, high.T], 1), cat([low, low.T], 1)], 0),
                preferred_element_type=F32,
            )
            g = both[0:8, :128] + both[8:16, :128] + both[16:24, :128]
            h = both[24:32, 128:] + both[32:40, 128:] + both[40:48, 128:]
            on = (p >= 0) & (p < count)
            on_far = (0.5 * g[:4] - (ROOT * xb) * g[5:6]) * (SCALE * xb[3:4])
            on_near = (h[:4] - (ROOT * xa) * h[7:8]) * (SCALE * xa[3:4])
            found.append((a, b, jnp.where(on, on_near, 0.0), jnp.where(on, on_far, 0.0)))
        for a, b, on_near, on_far in found:
            acc_ref[a] += on_near
            acc_ref[b] += on_far

    def turn(i, _):
        for v in range(3):
            t = 3 * i + v
            prepare(t, v)
            strengths((v + 2) % 3)
            sums(t - 2, (v + 1) % 3)
        return 0

    steps = (count + GROUP - 1) // GROUP + 2
    lax.fori_loop(0, (steps + 2) // 3, turn, 0)


def return_kernel(acc_ref, pret_ref, gret_ref, send, recv):
    n_own = pret_ref.shape[0]
    per = gret_ref.shape[0] // 4
    greet()
    copies = [
        pltpu.make_async_remote_copy(
            src_ref=acc_ref.at[pl.ds(n_own, n_own)],
            dst_ref=pret_ref,
            send_sem=send.at[0],
            recv_sem=recv.at[0],
            device_id={"slab": 1 - lax.axis_index("slab")},
            device_id_type=MESH,
        )
    ]
    for k in range(4):
        copies.append(
            pltpu.make_async_remote_copy(
                src_ref=acc_ref.at[pl.ds(2 * n_own + per * k, per)],
                dst_ref=gret_ref.at[pl.ds(per * k, per)],
                send_sem=send.at[1 + k],
                recv_sem=recv.at[1 + k],
                device_id={"dom": neighbour(k ^ 1)},
                device_id_type=MESH,
            )
        )
    for copy in copies:
        copy.start()
    for copy in copies:
        copy.wait()


def finish_kernel(ghost_ref, pool_ref, vel_ref, acc_ref, pret_ref, gret_ref, npos_ref, nvel_ref, total):
    n_own = vel_ref.shape[0]
    per = ghost_ref.shape[1]
    total[...] = acc_ref[0:n_own] + pret_ref[...]

    def back(i, _):
        for k in range(4):
            for u in range(4):
                total[ghost_ref[k, 4 * i + u]] += gret_ref[per * k + 4 * i + u]
        return 0

    lax.fori_loop(0, per // 4, back, 0)

    def write(i, _):
        for u in range(16):
            b = i * 16 + u
            lanes = pl.ds(pl.multiple_of(b * 128, 128), 128)
            npos_ref[:, lanes] = pool_ref[b, 0:3, :]
            nvel_ref[:, lanes] = vel_ref[b] + total[b, 0:3, :]
        return 0

    lax.fori_loop(0, n_own // 16, write, 0)


def shards(positions, velocities, destination, live_count, ghost_list, pair_blocks, pair_count):
    n_rows = positions.shape[1]
    n_groups = n_rows // BLOCK
    n_own = n_groups + TAIL
    n_ghost = 4 * ghost_list.shape[2]
    n_pool = 2 * n_own + n_ghost
    smem = pl.BlockSpec(memory_space=pltpu.SMEM)
    vmem = pl.BlockSpec(memory_space=pltpu.VMEM)
    anywhere = pl.BlockSpec(memory_space=pl.ANY)
    ghosts = ghost_list[0]
    pairs = pair_blocks[0].T

    pool, vel = pl.pallas_call(
        exchange_kernel,
        out_shape=(
            jax.ShapeDtypeStruct((n_pool, 4, BLOCK), F32),
            jax.ShapeDtypeStruct((n_own, 3, BLOCK), F32),
        ),
        in_specs=[anywhere, anywhere, anywhere, smem, smem],
        out_specs=(vmem, vmem),
        scratch_shapes=[
            pltpu.VMEM((3, n_rows), F32),
            pltpu.VMEM((3, n_rows), F32),
            pltpu.VMEM((n_groups, BLOCK), jnp.int32),
            pltpu.VMEM((n_own, 4, BLOCK), F32),
            pltpu.VMEM((6, n_groups, 2 * BLOCK), BF),
            pltpu.VMEM((3, n_groups, BLOCK), BF),
            pltpu.VMEM((4, BLOCK, n_groups), BF),
            pltpu.VMEM((4, 2, n_groups, BLOCK), F32),
            pltpu.VMEM((TAIL, 8, BLOCK), F32),
            pltpu.VMEM((TAIL, 8, BLOCK), F32),
            pltpu.VMEM((n_ghost, 4, BLOCK), F32),
            pltpu.SemaphoreType.DMA((3,)),
            pltpu.SemaphoreType.DMA((10,)),
            pltpu.SemaphoreType.DMA((10,)),
        ],
        compiler_params=pltpu.CompilerParams(
            collective_id=0, has_side_effects=True, vmem_limit_bytes=32 << 20
        ),
        name="exchange",
    )(positions, velocities, destination.reshape(n_groups, BLOCK), live_count, ghosts)

    acc = pl.pallas_call(
        pair_kernel,
        out_shape=jax.ShapeDtypeStruct((n_pool, 4, BLOCK), F32),
        in_specs=[smem, smem, vmem],
        out_specs=vmem,
        scratch_shapes=[
            pltpu.VMEM((3, GROUP // 2, BLOCK, 96), BF),
            pltpu.VMEM((3, GROUP // 2, 96, 2 * BLOCK), BF),
            pltpu.VMEM((3, GROUP, 48, BLOCK), BF),
            pltpu.VMEM((3, BLOCK, GROUP * BLOCK), BF),
            pltpu.VMEM((3, BLOCK, GROUP * BLOCK), BF),
        ],
        compiler_params=pltpu.CompilerParams(vmem_limit_bytes=32 << 20),
        name="pairs",
    )(pairs, pair_count, pool)

    pret, gret = pl.pallas_call(
        return_kernel,
        out_shape=(
            jax.ShapeDtypeStruct((n_own, 4, BLOCK), F32),
            jax.ShapeDtypeStruct((n_ghost, 4, BLOCK), F32),
        ),
        in_specs=[vmem],
        out_specs=(vmem, vmem),
        scratch_shapes=[pltpu.SemaphoreType.DMA((5,)), pltpu.SemaphoreType.DMA((5,))],
        compiler_params=pltpu.CompilerParams(
            collective_id=1, has_side_effects=True, vmem_limit_bytes=16 << 20
        ),
        name="returns",
    )(acc)

    return pl.pallas_call(
        finish_kernel,
        out_shape=(
            jax.ShapeDtypeStruct((3, n_own * BLOCK), F32),
            jax.ShapeDtypeStruct((3, n_own * BLOCK), F32),
        ),
        in_specs=[smem, vmem, vmem, vmem, vmem, vmem],
        out_specs=(vmem, vmem),
        scratch_shapes=[pltpu.VMEM((n_own, 4, BLOCK), F32)],
        compiler_params=pltpu.CompilerParams(vmem_limit_bytes=32 << 20),
        name="finish",
    )(ghosts, pool, vel, acc, pret, gret)


def solution(mesh):
    return jax.shard_map(
        shards,
        mesh=mesh,
        in_specs=(
            P(None, ("dom", "slab")),
            P(None, ("dom", "slab")),
            P(("dom", "slab")),
            P(("dom", "slab")),
            P(("dom", "slab"), None, None),
            P(("dom", "slab"), None, None),
            P(("dom", "slab")),
        ),
        out_specs=(P(None, ("dom", "slab")), P(None, ("dom", "slab"))),
        check_vma=False,
    )
```

time: 85 us -> 72.9 us (0.86)
  Pallas kernels: 73.8 us -> 66.4 us
  local copies, waits for them, and re-layouts: 8.87 us -> 4.34 us
    pallas_call x1, Pallas kernels: 19.6 us -> 13.4 us  [shards(): pl.pallas_call(pair_kernel, out_shape=jax.ShapeDtypeStruct((n_pool, 4, BL...]
    pallas_call x2, Pallas kernels: 36.9 us -> 31.7 us  [the longest x1 29.1 us: shards(): pl.pallas_call(exchange_kernel, out_shape=(jax.ShapeDtypeStruct((n_pool,...]
    pallas_call x1, Pallas kernels: 17.3 us -> 21.3 us  [shards(): pl.pallas_call(return_kernel, out_shape=(jax.ShapeDtypeStruct((n_own, 4,...]
    unnamed x15 -> x10, local copies, waits for them, and re-layouts: 8.11 us -> 4.34 us
where the time goes in v1:
time: 72.9 us; the launch traced here: 72.7 us
  Pallas kernels  66.4 us (91%)
  local copies, waits for them, and re-layouts  4.34 us (6%)
  between operations  1.97 us (3%)
    pallas_call x1, Pallas kernels, shards(): pl.pallas_call(exchange_kernel, out_shape=(jax.ShapeDtypeStruct((n_pool,...  29.1 us
    pallas_call x1, Pallas kernels, shards(): pl.pallas_call(return_kernel, out_shape=(jax.ShapeDtypeStruct((n_own, 4,...  21.3 us
    pallas_call x1, Pallas kernels, shards(): pl.pallas_call(pair_kernel, out_shape=jax.ShapeDtypeStruct((n_pool, 4, BL...  13.4 us
    unnamed x10, local copies, waits for them, and re-layouts  4.34 us
    pallas_call x1, Pallas kernels, shards(): pl.pallas_call(finish_kernel, out_shape=(jax.ShapeDtypeStruct((3, n_own *...  2.6 us

profile of v1, /device:TPU:1, one launch (start us, length us, event | category | flops | bytes accessed | tf_op | source)
XLA Modules:
  0.0 72.7 jit_solution(2589330680609473632)
XLA Ops:
  1.9 0.0 copy-start
  1.9 1.0 %copy-done = f32[3,32768]{1,0:T(4,128)S(1)} copy-done((f32[3,32768]{1,0:T(4,128)S(1)}, f32[3,32768]{1,0:T(4,128)}, u32[]{:S(2)}) %copy-start) | copy-done | bytes 393240
  3.0 0.0 copy-start.1
  3.0 1.0 %copy-done.1 = f32[3,32768]{1,0:T(4,128)S(1)} copy-done((f32[3,32768]{1,0:T(4,128)S(1)}, f32[3,32768]{1,0:T(4,128)}, u32[]{:S(2)}) %copy-start.1) | copy-done | bytes 393240
  4.0 0.0 copy-start.2
  4.0 0.9 %copy-done.2 = s32[32768]{0:T(1024)S(1)} copy-done((s32[32768]{0:T(1024)S(1)}, s32[32768]{0:T(1024)}, u32[]{:S(2)}) %copy-start.2) | copy-done | bytes 131096
  4.9 0.0 copy-start.3
  4.9 0.7 copy-done.3
  5.6 29.1 %exchange.1 = (f32[672,4,128]{2,1,0:T(4,128)S(1)}, f32[272,3,128]{2,1,0:T(4,128)S(1)}) custom-call(f32[3,32768]{1,0:T(4,128)S(1)} %copy-done, f32[3,32768]{1,0:T(4,128)S(1)} %copy-done.1, s32[256,128]{1,0:T(8,128)S(1)} %bitcast.5, s32[1]{0:T(128)S(6)} %copy.9.live_ref, s32[4,32]{1,0:T(4,128)S(1)} %bitcast.6), custom_call_target="tpu_custom_call" | custom-call | tf_op jit(solution)/shard_map/exchange/pallas_call | solution.py:347
  34.7 0.0 copy-start.4
  34.7 0.7 copy-done.4
  35.4 13.4 %pairs.1.acc_ref = f32[672,4,128]{2,1,0:T(4,128)S(1)} custom-call(s32[2,512]{1,0:T(2,128)S(1)} %bitcast.8, s32[1]{0:T(128)S(6)} %copy.10.count_ref, f32[672,4,128]{2,1,0:T(4,128)S(1)} %get-tuple-element.6.pool.pool_ref), custom_call_target="tpu_custom_call" | custom-call | tf_op jit(solution)/shard_map/pairs/pallas_call | solution.py:377
  48.8 21.3 %returns.1 = (f32[272,4,128]{2,1,0:T(4,128)S(1)}, f32[128,4,128]{2,1,0:T(4,128)S(1)}) custom-call(f32[672,4,128]{2,1,0:T(4,128)S(1)} %pairs.1.acc_ref), custom_call_target="tpu_custom_call" | custom-call | tf_op jit(solution)/shard_map/returns/pallas_call | solution.py:393
  70.1 2.6 %finish.1 = (f32[3,34816]{1,0:T(4,128)}, f32[3,34816]{1,0:T(4,128)}) custom-call(s32[4,32]{1,0:T(4,128)S(1)} %bitcast.7, f32[672,4,128]{2,1,0:T(4,128)S(1)} %get-tuple-element.6.pool.pool_ref, f32[272,3,128]{2,1,0:T(4,128)S(1)} %get-tuple-element.7.vel_ref, f32[672,4,128]{2,1,0:T(4,128)S(1)} %pairs.1.acc_ref, f32[272,4,128]{2,1,0:T(4,128)S(1)} %get-tuple-element.8.pret_ref, ...), custom_call_target="tpu_custom_call" | custom-call | tf_op jit(solution)/shard_map/finish/pallas_call | solution.py:408
Async XLA Ops:
  1.9 1.0 %copy-start = (f32[3,32768]{1,0:T(4,128)S(1)}, f32[3,32768]{1,0:T(4,128)}, u32[]{:S(2)}) copy-start(f32[3,32768]{1,0:T(4,128)} %pos_hbm.1) | copy-start | bytes 1179652
  3.0 1.0 %copy-start.1 = (f32[3,32768]{1,0:T(4,128)S(1)}, f32[3,32768]{1,0:T(4,128)}, u32[]{:S(2)}) copy-start(f32[3,32768]{1,0:T(4,128)} %vel_hbm.1) | copy-start | bytes 1179652
  4.0 0.9 %copy-start.2 = (s32[32768]{0:T(1024)S(1)}, s32[32768]{0:T(1024)}, u32[]{:S(2)}) copy-start(s32[32768]{0:T(1024)} %param.9) | copy-start | bytes 393220
  4.9 0.7 copy-start.3
  34.7 0.7 copy-start.4

commit v2 on v1

--- a/solution.py
+++ b/solution.py
@@ -47,9 +47,10 @@
 
 
 def exchange_kernel(
-    pos_hbm, vel_hbm, dest_hbm, live_ref, ghost_ref,
-    pool_ref, vout_ref,
-    pos_ref, vel_ref, dest_ref, own, main, extra, ranks, spans, moved, landed, gbuf, local, send, recv,
+    pos_hbm, vel_hbm, dest_hbm, pairs_hbm, ghost_hbm, live_ref, count_ref,
+    pool_ref, xst_ref, vst_ref, mine_ref, theirs_ref,
+    pos_ref, vel_ref, dest_ref, pairs_ref, ghost_ref, own, drifted, speeds,
+    main, extra, ranks, spans, moved, landed, gbuf, local, send, recv,
 ):
     n_groups = dest_ref.shape[0]
     n_own = own.shape[0]
@@ -57,7 +58,13 @@
     partner = {"slab": 1 - lax.axis_index("slab")}
     live = live_ref[0]
     loads = []
-    for i, (source, target) in enumerate(((dest_hbm, dest_ref), (pos_hbm, pos_ref), (vel_hbm, vel_ref))):
+    for i, (source, target) in enumerate((
+        (dest_hbm, dest_ref),
+        (pos_hbm, pos_ref.at[0:3]),
+        (vel_hbm, vel_ref.at[0:3]),
+        (pairs_hbm, pairs_ref),
+        (ghost_hbm, ghost_ref),
+    )):
         loads.append(pltpu.make_async_copy(source, target, local.at[i]))
         loads[-1].start()
     greet()
@@ -68,40 +75,36 @@
         slot = slot + lax.broadcasted_iota(jnp.int32, (size, 128), 1)
         return jnp.where(slot < live, codes, -1)
 
-    row16 = lax.broadcasted_iota(jnp.int32, (16, 128), 0)
+    row4 = lax.broadcasted_iota(jnp.int32, (4, 128), 0)
 
     def drift(i, _):
         base = pl.multiple_of(i * 16, 16)
         stay = jnp.where(codes_of(base, 16) == 0, 1.0, 0.0)
         for u in range(16):
             lanes = pl.ds(pl.multiple_of((base + u) * 128, 128), 128)
-            p = pos_ref[:, lanes]
+            rows = pl.ds(pl.multiple_of((base + u) * 8, 8), 4)
             v = vel_ref[:, lanes]
+            x = pos_ref[:, lanes] + step_size * v
             here = stay[u : u + 1]
-            kept = (p + step_size * v) * here
-            own[base + u, 0:3, :] = kept
-            own[base + u, 3:4, :] = here
-            pool_ref[base + u, 0:3, :] = kept
-            pool_ref[base + u, 3:4, :] = here
-            vout_ref[base + u] = v * here
+            own[base + u] = jnp.where(row4 == 3, 1.0, x) * here
+            vst_ref[:, lanes] = v[0:3] * here
+            drifted[rows, :] = x
+            speeds[rows, :] = v
         for c in range(3):
-            p = jnp.zeros((16, 128), F32)
-            v = jnp.zeros((16, 128), F32)
-            for u in range(16):
-                lanes = pl.ds(pl.multiple_of((base + u) * 128, 128), 128)
-                p = jnp.where(row16 == u, pos_ref[c : c + 1, lanes], p)
-                v = jnp.where(row16 == u, vel_ref[c : c + 1, lanes], v)
-            high, middle, low = split3(p + step_size * v)
+            column = pl.ds(base * 8 + c, 16, stride=8)
+            high, middle, low = split3(drifted[column, :])
             main[c, pl.ds(base, 16), 0:128] = high.astype(BF)
             main[c, pl.ds(base, 16), 128:256] = middle.astype(BF)
             extra[c, pl.ds(base, 16), :] = low.astype(BF)
-            high, middle, _ = split3(v)
+            high, middle, _ = split3(speeds[column, :])
             main[3 + c, pl.ds(base, 16), 0:128] = high.astype(BF)
             main[3 + c, pl.ds(base, 16), 128:256] = middle.astype(BF)
         return 0
 
     for load in loads:
         load.wait()
+    mine_ref[0:2, :] = pairs_ref[...]
+    mine_ref[2:4, :] = jnp.full((2, mine_ref.shape[1]), count_ref[0], jnp.int32)
     lax.fori_loop(0, n_groups // 16, drift, 0)
 
     def remote(source, target, slot, device):
@@ -116,6 +119,10 @@
 
     body = remote(own.at[pl.ds(0, n_groups)], pool_ref.at[pl.ds(n_own, n_groups)], 0, partner)
     body.start()
+    listed = remote(mine_ref, theirs_ref, 10, partner)
+    listed.start()
+    kept = pltpu.make_async_copy(own.at[pl.ds(0, n_groups)], pool_ref.at[pl.ds(0, n_groups)], local.at[5])
+    kept.start()
 
     codes = codes_of(0, n_groups)
     lane_r = lax.broadcasted_iota(jnp.int32, (128, 256), 0)
@@ -172,7 +179,7 @@
     for j in range(TAIL):
         own[n_groups + j] = landed[j, 0:4, :]
         pool_ref[n_groups + j] = landed[j, 0:4, :]
-        vout_ref[n_groups + j] = landed[j, 4:7, :]
+        vst_ref[:, (n_groups + j) * 128 : (n_groups + j) * 128 + 128] = landed[j, 4:7, :]
     tail = remote(own.at[pl.ds(n_groups, TAIL)], pool_ref.at[pl.ds(n_own + n_groups, TAIL)], 5, partner)
     tail.start()
     per = n_ghost // 4
@@ -188,10 +195,16 @@
         there = pl.ds(2 * n_own + per * k, per)
         ghosts.append(remote(gbuf.at[pl.ds(per * k, per)], pool_ref.at[there], 6 + k, {"dom": neighbour(k)}))
         ghosts[-1].start()
-    for copy in ghosts:
+
+    def stage(i, _):
+        for u in range(16):
+            lanes = pl.ds(pl.multiple_of((16 * i + u) * 128, 128), 128)
+            xst_ref[:, lanes] = own[16 * i + u, 0:3, :]
+        return 0
+
+    lax.fori_loop(0, n_own // 16, stage, 0)
+    for copy in (*ghosts, body, listed, tail, kept):
         copy.wait()
-    body.wait()
-    tail.wait()
 
 
 def features(block, row):
@@ -199,19 +212,76 @@
     return pos, jnp.sum(pos * pos, axis=0, keepdims=True), block[3:4]
 
 
-def pair_kernel(pairs_ref, count_ref, pool, acc_ref, lefts, rights, nears, highs, lows):
+def share_pairs(mine, theirs, work, n_own):
+    here, there = mine[2, 0], theirs[2, 0]
+    extra = jnp.abs(here - there) // 2
+
+    def copy(i, _):
+        for u in range(8):
+            for side in range(2):
+                work[side, 8 * i + u] = mine[side, 8 * i + u]
+        return 0
+
+    lax.fori_loop(0, (here + 7) // 8, copy, 0)
+
+    def more(state):
+        p, moved, _ = state
+        return (moved < extra) & (p > 0)
+
+    def give(state):
+        p, moved, free = state
+        for _ in range(8):
+            at = jnp.maximum(p - 1, 0)
+            a, b = work[0, at], work[1, at]
+            gone = ((b < 2 * n_own) & (moved < extra)) | (p <= 0)
+            keep = jnp.where(gone, work.shape[1] - 1, free - 1)
+            work[0, keep] = a
+            work[1, keep] = b
+            moved = moved + jnp.where(gone & (p > 0), 1, 0)
+            free = jnp.where(gone, free, free - 1)
+            p = jnp.maximum(p - 1, 0)
+        return p, moved, free
+
+    def take(state):
+        p, moved, end = state
+        for _ in range(8):
+            at = jnp.maximum(p - 1, 0)
+            a, b = theirs[0, at], theirs[1, at]
+            ours = (b < 2 * n_own) & (moved < extra) & (p > 0)
+            work[0, end] = a + n_own
+            work[1, end] = jnp.where(b < n_own, b + n_own, b - n_own)
+            moved = moved + jnp.where(ours, 1, 0)
+            end = end + jnp.where(ours, 1, 0)
+            p = jnp.maximum(p - 1, 0)
+        return p, moved, end
+
+    def giver():
+        p, moved, free = lax.while_loop(more, give, (here, jnp.int32(0), here))
+        return here - moved, p, free - p
+
+    def taker():
+        _, _, end = lax.while_loop(more, take, (there, jnp.int32(0), here))
+        return end, end, jnp.int32(0)
+
+    return lax.cond(here > there, giver, taker)
+
+
+def pair_kernel(mine, theirs, pool, xst_ref, acc_ref, npos_ref, lefts, rights, nears, highs, lows, work, sem):
+    n_own = xst_ref.shape[1] // 128
+    staged = pltpu.make_async_copy(xst_ref, npos_ref, sem.at[0])
+    staged.start()
     acc_ref[...] = jnp.zeros_like(acc_ref)
     rights[...] = jnp.zeros_like(rights)
+    count, turn_at, skip = share_pairs(mine, theirs, work, n_own)
     row = lax.broadcasted_iota(jnp.int32, (8, 128), 0)
-    count = count_ref[0]
-    npair = pairs_ref.shape[1]
 
     def cat(parts, axis):
         return jnp.concatenate(parts, axis=axis)
 
     def blocks_of(p):
-        p = jnp.clip(p, 0, npair - 1)
-        return pairs_ref[0, p], pairs_ref[1, p]
+        p = jnp.clip(p, 0, count - 1)
+        p = p + jnp.where(p >= turn_at, skip, 0)
+        return work[0, p], work[1, p]
 
     def prepare(t, slot):
         left = []
@@ -275,6 +345,7 @@
 
     steps = (count + GROUP - 1) // GROUP + 2
     lax.fori_loop(0, (steps + 2) // 3, turn, 0)
+    staged.wait()
 
 
 def return_kernel(acc_ref, pret_ref, gret_ref, send, recv):
@@ -308,28 +379,26 @@
         copy.wait()
 
 
-def finish_kernel(ghost_ref, pool_ref, vel_ref, acc_ref, pret_ref, gret_ref, npos_ref, nvel_ref, total):
-    n_own = vel_ref.shape[0]
+def finish_kernel(ghost_ref, vst_ref, acc_ref, pret_ref, gret_ref, nvel_ref):
     per = ghost_ref.shape[1]
-    total[...] = acc_ref[0:n_own] + pret_ref[...]
-
-    def back(i, _):
-        for k in range(4):
-            for u in range(4):
-                total[ghost_ref[k, 4 * i + u]] += gret_ref[per * k + 4 * i + u]
-        return 0
-
-    lax.fori_loop(0, per // 4, back, 0)
 
     def write(i, _):
         for u in range(16):
             b = i * 16 + u
             lanes = pl.ds(pl.multiple_of(b * 128, 128), 128)
-            npos_ref[:, lanes] = pool_ref[b, 0:3, :]
-            nvel_ref[:, lanes] = vel_ref[b] + total[b, 0:3, :]
-        return 0
-
-    lax.fori_loop(0, n_own // 16, write, 0)
+            nvel_ref[:, lanes] = vst_ref[:, lanes] + (acc_ref[b, 0:3, :] + pret_ref[b, 0:3, :])
+        return 0
+
+    lax.fori_loop(0, pret_ref.shape[0] // 16, write, 0)
+
+    def back(i, _):
+        for k in range(4):
+            for u in range(8):
+                lanes = pl.ds(pl.multiple_of(ghost_ref[k, 8 * i + u] * 128, 128), 128)
+                nvel_ref[:, lanes] += gret_ref[per * k + 8 * i + u, 0:3, :]
+        return 0
+
+    lax.fori_loop(0, per // 8, back, 0)
 
 
 def shards(positions, velocities, destination, live_count, ghost_list, pair_blocks, pair_count):
@@ -340,23 +409,31 @@
     n_pool = 2 * n_own + n_ghost
     smem = pl.BlockSpec(memory_space=pltpu.SMEM)
     vmem = pl.BlockSpec(memory_space=pltpu.VMEM)
-    anywhere = pl.BlockSpec(memory_space=pl.ANY)
+    hbm = pl.BlockSpec(memory_space=pltpu.HBM)
     ghosts = ghost_list[0]
     pairs = pair_blocks[0].T
-
-    pool, vel = pl.pallas_call(
+    lists = jax.ShapeDtypeStruct((4, pairs.shape[1]), jnp.int32)
+
+    pool, xst, vst, mine, theirs = pl.pallas_call(
         exchange_kernel,
         out_shape=(
             jax.ShapeDtypeStruct((n_pool, 4, BLOCK), F32),
-            jax.ShapeDtypeStruct((n_own, 3, BLOCK), F32),
+            jax.ShapeDtypeStruct((3, n_own * BLOCK), F32),
+            jax.ShapeDtypeStruct((3, n_own * BLOCK), F32),
+            lists,
+            lists,
         ),
-        in_specs=[anywhere, anywhere, anywhere, smem, smem],
-        out_specs=(vmem, vmem),
+        in_specs=[hbm, hbm, hbm, hbm, hbm, smem, smem],
+        out_specs=(vmem, vmem, vmem, vmem, vmem),
         scratch_shapes=[
-            pltpu.VMEM((3, n_rows), F32),
-            pltpu.VMEM((3, n_rows), F32),
+            pltpu.VMEM((4, n_rows), F32),
+            pltpu.VMEM((4, n_rows), F32),
             pltpu.VMEM((n_groups, BLOCK), jnp.int32),
+            pltpu.VMEM(pairs.shape, jnp.int32),
+            pltpu.SMEM(ghosts.shape, jnp.int32),
             pltpu.VMEM((n_own, 4, BLOCK), F32),
+            pltpu.VMEM((8 * n_groups, BLOCK), F32),
+            pltpu.VMEM((8 * n_groups, BLOCK), F32),
             pltpu.VMEM((6, n_groups, 2 * BLOCK), BF),
             pltpu.VMEM((3, n_groups, BLOCK), BF),
             pltpu.VMEM((4, BLOCK, n_groups), BF),
@@ -364,31 +441,36 @@
             pltpu.VMEM((TAIL, 8, BLOCK), F32),
             pltpu.VMEM((TAIL, 8, BLOCK), F32),
             pltpu.VMEM((n_ghost, 4, BLOCK), F32),
-            pltpu.SemaphoreType.DMA((3,)),
-            pltpu.SemaphoreType.DMA((10,)),
-            pltpu.SemaphoreType.DMA((10,)),
+            pltpu.SemaphoreType.DMA((6,)),
+            pltpu.SemaphoreType.DMA((11,)),
+            pltpu.SemaphoreType.DMA((11,)),
         ],
         compiler_params=pltpu.CompilerParams(
             collective_id=0, has_side_effects=True, vmem_limit_bytes=32 << 20
         ),
         name="exchange",
-    )(positions, velocities, destination.reshape(n_groups, BLOCK), live_count, ghosts)
-
-    acc = pl.pallas_call(
+    )(positions, velocities, destination.reshape(n_groups, BLOCK), pairs, ghosts, live_count, pair_count)
+
+    acc, new_positions = pl.pallas_call(
         pair_kernel,
-        out_shape=jax.ShapeDtypeStruct((n_pool, 4, BLOCK), F32),
-        in_specs=[smem, smem, vmem],
-        out_specs=vmem,
+        out_shape=(
+            jax.ShapeDtypeStruct((n_pool, 4, BLOCK), F32),
+            jax.ShapeDtypeStruct((3, n_own * BLOCK), F32),
+        ),
+        in_specs=[smem, smem, vmem, vmem],
+        out_specs=(vmem, hbm),
         scratch_shapes=[
             pltpu.VMEM((3, GROUP // 2, BLOCK, 96), BF),
             pltpu.VMEM((3, GROUP // 2, 96, 2 * BLOCK), BF),
             pltpu.VMEM((3, GROUP, 48, BLOCK), BF),
             pltpu.VMEM((3, BLOCK, GROUP * BLOCK), BF),
             pltpu.VMEM((3, BLOCK, GROUP * BLOCK), BF),
+            pltpu.SMEM((2, 2 * pairs.shape[1]), jnp.int32),
+            pltpu.SemaphoreType.DMA((1,)),
         ],
         compiler_params=pltpu.CompilerParams(vmem_limit_bytes=32 << 20),
         name="pairs",
-    )(pairs, pair_count, pool)
+    )(mine, theirs, pool, xst)
 
     pret, gret = pl.pallas_call(
         return_kernel,
@@ -405,18 +487,15 @@
         name="returns",
     )(acc)
 
-    return pl.pallas_call(
+    new_velocities = pl.pallas_call(
         finish_kernel,
-        out_shape=(
-            jax.ShapeDtypeStruct((3, n_own * BLOCK), F32),
-            jax.ShapeDtypeStruct((3, n_own * BLOCK), F32),
-        ),
-        in_specs=[smem, vmem, vmem, vmem, vmem, vmem],
-        out_specs=(vmem, vmem),
-        scratch_shapes=[pltpu.VMEM((n_own, 4, BLOCK), F32)],
+        out_shape=jax.ShapeDtypeStruct((3, n_own * BLOCK), F32),
+        in_specs=[smem, vmem, vmem, vmem, vmem],
+        out_specs=vmem,
         compiler_params=pltpu.CompilerParams(vmem_limit_bytes=32 << 20),
         name="finish",
-    )(ghosts, pool, vel, acc, pret, gret)
+    )(ghosts, vst, acc, pret, gret)
+    return new_positions, new_velocities
 
 
 def solution(mesh):

time: 72.9 us -> 74.3 us (1.019)
  the two profiles are of different devices: /device:TPU:1 before, /device:TPU:0 now
where the time goes in v2:
time: 74.3 us; the launch traced here: 74 us
  Pallas kernels  67.7 us (91%)
  local copies, waits for them, and re-layouts  4.35 us (6%)
  between operations  1.96 us (3%)
    pallas_call x1, Pallas kernels, shards(): pl.pallas_call(exchange_kernel, out_shape=(jax.ShapeDtypeStruct((n_pool,...  28 us
    pallas_call x1, Pallas kernels, shards(): pl.pallas_call(pair_kernel, out_shape=(jax.ShapeDtypeStruct((n_pool, 4, B...  27.4 us
    pallas_call x1, Pallas kernels, shards(): pl.pallas_call(return_kernel, out_shape=(jax.ShapeDtypeStruct((n_own, 4,...  9.96 us
    unnamed x10, local copies, waits for them, and re-layouts  4.35 us
    pallas_call x1, Pallas kernels, shards(): pl.pallas_call(finish_kernel, out_shape=jax.ShapeDtypeStruct((3, n_own *...  2.37 us

profile of v2, /device:TPU:0, one launch (start us, length us, event | category | flops | bytes accessed | tf_op | source)
XLA Modules:
  0.0 74.0 jit_solution(8940249862633083513)
XLA Ops:
  1.9 0.0 copy-start
  1.9 1.0 %copy-done = f32[3,32768]{1,0:T(4,128)S(1)} copy-done((f32[3,32768]{1,0:T(4,128)S(1)}, f32[3,32768]{1,0:T(4,128)}, u32[]{:S(2)}) %copy-start) | copy-done | bytes 393240
  3.0 0.0 copy-start.1
  3.0 1.0 %copy-done.1 = f32[3,32768]{1,0:T(4,128)S(1)} copy-done((f32[3,32768]{1,0:T(4,128)S(1)}, f32[3,32768]{1,0:T(4,128)}, u32[]{:S(2)}) %copy-start.1) | copy-done | bytes 393240
  4.0 0.0 copy-start.2
  4.0 0.9 %copy-done.2 = s32[32768]{0:T(1024)S(1)} copy-done((s32[32768]{0:T(1024)S(1)}, s32[32768]{0:T(1024)}, u32[]{:S(2)}) %copy-start.2) | copy-done | bytes 131096
  4.9 0.0 copy-start.3
  4.9 0.7 copy-done.3
  5.6 0.0 copy-start.4
  5.6 0.7 copy-done.4
  6.3 28.0 %exchange.1 = (f32[672,4,128]{2,1,0:T(4,128)S(1)}, f32[3,34816]{1,0:T(4,128)S(1)}, f32[3,34816]{1,0:T(4,128)S(1)}, s32[4,512]{1,0:T(4,128)S(1)}, s32[4,512]{1,0:T(4,128)S(1)}) custom-call(f32[3,32768]{1,0:T(4,128)S(1)} %copy-done, f32[3,32768]{1,0:T(4,128)S(1)} %copy-done.1, s32[256,128]{1,0:T(8,128)S(1)} %bitcast.5, s32[2,512]{1,0:T(2,128)S(1)} %bitcast.8, ...), custom_call_target="tpu_custom_call" | custom-call | tf_op jit(solution)/shard_map/exchange/pallas_call | solution.py:417
  34.2 27.4 %pairs.1 = (f32[672,4,128]{2,1,0:T(4,128)S(1)}, f32[3,34816]{1,0:T(4,128)}) custom-call(s32[4,512]{1,0:T(4,128)S(1)} %get-tuple-element.11.mine, s32[4,512]{1,0:T(4,128)S(1)} %get-tuple-element.12.theirs, f32[672,4,128]{2,1,0:T(4,128)S(1)} %get-tuple-element.13.pool, f32[3,34816]{1,0:T(4,128)S(1)} %get-tuple-element.14.xst_ref), custom_call_target="tpu_custom_call" | custom-call | tf_op jit(solution)/shard_map/pairs/pallas_call | solution.py:454
  61.7 10.0 %returns.1 = (f32[272,4,128]{2,1,0:T(4,128)S(1)}, f32[128,4,128]{2,1,0:T(4,128)S(1)}) custom-call(f32[672,4,128]{2,1,0:T(4,128)S(1)} %get-tuple-element.17.acc_ref), custom_call_target="tpu_custom_call" | custom-call | tf_op jit(solution)/shard_map/returns/pallas_call | solution.py:475
  71.7 2.4 %finish.1 = f32[3,34816]{1,0:T(4,128)} custom-call(s32[4,32]{1,0:T(4,128)S(1)} %bitcast.7, f32[3,34816]{1,0:T(4,128)S(1)} %get-tuple-element.16.vst_ref, f32[672,4,128]{2,1,0:T(4,128)S(1)} %get-tuple-element.17.acc_ref, f32[272,4,128]{2,1,0:T(4,128)S(1)} %get-tuple-element.18.pret_ref, f32[128,4,128]{2,1,0:T(4,128)S(1)} %get-tuple-element.19.gret_ref), custom_call_target="tpu_custom_call" | custom-call | tf_op jit(solution)/shard_map/finish/pallas_call | solution.py:490
Async XLA Ops:
  1.9 1.0 %copy-start = (f32[3,32768]{1,0:T(4,128)S(1)}, f32[3,32768]{1,0:T(4,128)}, u32[]{:S(2)}) copy-start(f32[3,32768]{1,0:T(4,128)} %pos_hbm.1) | copy-start | bytes 1179652
  3.0 1.0 %copy-start.1 = (f32[3,32768]{1,0:T(4,128)S(1)}, f32[3,32768]{1,0:T(4,128)}, u32[]{:S(2)}) copy-start(f32[3,32768]{1,0:T(4,128)} %vel_hbm.1) | copy-start | bytes 1179652
  4.0 0.9 %copy-start.2 = (s32[32768]{0:T(1024)S(1)}, s32[32768]{0:T(1024)}, u32[]{:S(2)}) copy-start(s32[32768]{0:T(1024)} %param.9) | copy-start | bytes 393220
  4.9 0.7 copy-start.3
  5.6 0.7 copy-start.4
